TPU v7x, 768 devices: a whole 4x8x12 slice. The times are simulated.
768 devices in a mesh: dp: 96 (over y_hi, x, z), tensor: 8 (over y_lo, core).
Axes of the slice: x: 4, y: 8 (y_hi: 2, y_lo: 4; y = y_hi * 4 + y_lo), z: 12, core: 2. Of those that a mesh axis runs over, the one named last changes fastest.
Arguments:
- gradient: bfloat16 [96, 2, 128, 14336], P('dp', None, None, 'tensor'), may hold values from -6 to 6
- error_buffer: float32 [96, 2, 128, 14336], P('dp', None, None, 'tensor'), may hold values from -4 to 4
- q_warm: float32 [2, 14336, 64], P(None, 'tensor'), may hold values from -0.046875 to 0.046875
Outputs:
- new_error: float32 [96, 2, 128, 14336], P('dp', None, None, 'tensor')
- p_factor: float32 [2, 128, 64], replicated
- q_factor: float32 [2, 14336, 64], P(None, 'tensor')
All inputs are finite; a program needn't handle non-finite values.
Results may differ from a plain program's by a relative error of at most 0.0003.
Values sent between devices are 32-bit elements; how exact they have to be, the bound alone decides.
A program may use at most 32 MiB of HBM per device.

v0:
```python
import jax
import jax.numpy as jnp
from jax import lax
from jax.sharding import PartitionSpec as P


def gram_of(block):
    return jnp.einsum("knr,kns->krs", block, block, precision=lax.Precision.HIGHEST)


def apply_inverse(lower, block):

    def single(low, part):
        return jax.scipy.linalg.solve_triangular(low, part.T, lower=True).T

    return jax.vmap(single)(lower, block)


def local(gradient, error_buffer, q_warm):
    corrected = gradient[0].astype(jnp.float32) + error_buffer[0]
    p_local = jnp.einsum("knf,kfr->knr", corrected, q_warm, precision=lax.Precision.HIGHEST)
    p_sum = lax.psum(p_local, ("dp", "tensor"))
    lower = jnp.linalg.cholesky(gram_of(p_sum))
    p_factor = apply_inverse(lower, p_sum)
    q_local = jnp.einsum("knf,knr->kfr", corrected, p_factor, precision=lax.Precision.HIGHEST)
    q_factor = lax.psum(q_local, "dp")
    replicas = lax.axis_size("dp")
    decompressed = (
        jnp.einsum("knr,kfr->knf", p_factor, q_factor, precision=lax.Precision.HIGHEST) / replicas
    )
    new_error = (corrected - decompressed)[None]
    return (new_error, p_factor, q_factor)


def solution(mesh):
    in_specs = (
        P("dp", None, None, "tensor"),
        P("dp", None, None, "tensor"),
        P(None, "tensor", None),
    )
    out_specs = (P("dp", None, None, "tensor"), P(), P(None, "tensor", None))
    return jax.shard_map(local, mesh=mesh, in_specs=in_specs, out_specs=out_specs, check_vma=False)
```

profile of v0, /device:TPU:56, one launch (start us, length us, event | category | flops | bytes accessed | tf_op | source)
XLA Modules:
  0.0 1701.1 jit_solution(17570641564609822935)
XLA Ops:
  7.2 0.0 copy-start
  7.2 0.0 copy-start.1
  7.2 0.0 all-reduce.3.cloned.1.call-start
  7.2 1.1 copy-done
  8.3 4.6 fusion.4
  12.9 0.0 all-reduce.3.cloned.1.call-update
  13.0 0.0 all-reduce.5.cloned.1.call-start
  13.0 456.8 %all-reduce.3.cloned.1.call-done = f32[2,128,64]{1,2,0:T(8,128)} async-done(((f32[2,128,64]{1,2,0:T(8,128)}), f32[2,128,64]{1,2,0:T(8,128)}) %all-reduce.3.cloned.1.call-update) | async-done | bytes 65552 | tf_op jit(solution)/shard_map/psum | solution.py:22
  469.9 1.1 fusion.9
  471.0 0.1 copy.8
  471.1 11.7 custom-call.8
  482.9 0.1 compare_reduce_fusion
  483.0 0.1 select_bitcast_fusion
  483.1 9.8 custom-call.9
  492.9 1.1 fusion.6
  494.1 0.0 copy-done.1
  494.1 0.0 copy-start.3
  494.1 3.4 fusion.2
  497.5 0.0 all-reduce.5.cloned.1.call-update
  497.5 1191.2 %all-reduce.5.cloned.1.call-done = f32[2,1792,64]{1,2,0:T(8,128)} async-done(((f32[2,1792,64]{1,2,0:T(8,128)}), f32[2,1792,64]{1,2,0:T(8,128)}) %all-reduce.5.cloned.1.call-update) | async-done | bytes 917520 | tf_op jit(solution)/shard_map/psum | solution.py:26
  1688.7 0.0 copy-done.3
  1688.8 0.0 copy-start.2
  1688.8 4.6 fusion.1
  1693.3 0.0 copy-done.2
  1693.3 0.9 copy.13
  (4 shorter events, 0.1 us)
Async XLA Ops:
  7.2 1.2 copy-start
  7.2 486.9 %copy-start.1 = (f32[1,2,128,1792]{3,2,1,0:T(8,128)S(1)}, f32[1,2,128,1792]{3,2,1,0:T(8,128)}, u32[]{:S(2)}) copy-start(f32[1,2,128,1792]{3,2,1,0:T(8,128)} %param.4) | copy-start | bytes 5505028
  7.2 462.7 %all-reduce.3.cloned.1.call-start = ((), (), s32[]{:S(2)}) async-start(), calls=%async_computation | async-start | bytes 131072 | tf_op jit(solution)/shard_map/psum | solution.py:22
  13.0 1675.8 %all-reduce.5.cloned.1.call-start = ((), (), s32[]{:S(2)}) async-start(), calls=%async_computation.1 | async-start | bytes 1835008 | tf_op jit(solution)/shard_map/psum | solution.py:26
  494.1 1194.7 %copy-start.3 = (f32[2,64,128]{2,1,0:T(8,128)}, f32[2,64,128]{2,1,0:T(8,128)S(1)}, u32[]{:S(2)}) copy-start(f32[2,64,128]{2,1,0:T(8,128)S(1)} %fusion.6) | copy-start | bytes 196612
  1688.8 4.6 copy-start.2
Sparse Core Ops, SparseCore 0:
  14.0 455.8 all-reduce.2
  497.6 1191.0 all-reduce.4
where the time goes:
time: 1700 us
  waiting for transfers between devices  1650 us (97%)
  other arithmetic  21.8 us (1%)
    psum x1, waiting for transfers between devices, local(): q_factor = lax.psum(q_local, 'dp')  1190 us
    psum x1, waiting for transfers between devices, local(): p_sum = lax.psum(p_local, ('dp', 'tensor'))  457 us
  transfers between devices with their start and end apart: 2, of which 2 were waited for; matrix products, arithmetic and copies ran while one was open for 0% of the time, Pallas kernels for 0%

commit v1 on v0

v1 whole, which is shorter than its diff:
```python
import functools

import jax
import jax.numpy as jnp
from jax import lax
from jax.experimental import pallas as pl
from jax.experimental.pallas import tpu as pltpu
from jax.sharding import PartitionSpec as P

HI = lax.Precision.HIGHEST
NX, NZ, NYL = 4, 12, 4
NY = 2 * NYL
FD = 1792
UNITS = 56
CH = 5
QU = NZ * CH
FAR_FIRST = (6, 5, 7, 4, 8, 3, 9, 2, 10, 1, 11, 0)
NEAR_FIRST = (1, 11, 2, 10, 3, 9, 4, 8, 5, 7, 6)
NT = (((1,), (1,)), ((), ()))


def dot(a, b):
    return jnp.dot(a, b, precision=HI, preferred_element_type=jnp.float32)


def dot_nt(a, b):
    return lax.dot_general(a, b, NT, precision=HI, preferred_element_type=jnp.float32)


def halves(a):
    hi = a.astype(jnp.bfloat16)
    return hi, (a - hi.astype(jnp.float32)).astype(jnp.bfloat16)


def dot3(a, b):
    (ah, al), (bh, bl) = a, halves(b)
    f = functools.partial(jnp.dot, preferred_element_type=jnp.float32)
    return f(ah, bh) + (f(ah, bl) + f(al, bh))


def inverse_factors(grams):
    rows = lax.broadcasted_iota(jnp.int32, (8, 128), 0)
    lanes = lax.broadcasted_iota(jnp.int32, (8, 128), 1)
    ms = []
    for g in grams:
        blocks = []
        for b in range(8):
            eye = jnp.where(lanes[:, :64] == rows[:, :64] + 8 * b, 1.0, 0.0)
            blocks.append(jnp.concatenate([g[8 * b : 8 * b + 8], eye.astype(jnp.float32)], axis=1))
        ms.append(blocks)
    for j in range(63):
        jb, ji = divmod(j, 8)
        for m in ms:
            row = m[jb][ji : ji + 1]
            scaled = row / row[:, j : j + 1]
            for b in range(jb, 8):
                col = m[b][:, j : j + 1]
                if b == jb:
                    col = jnp.where(rows[:, :1] > ji, col, 0.0)
                m[b] = m[b] - col * scaled
    out = []
    for m in ms:
        parts = []
        for b in range(8):
            d = jnp.sum(jnp.where(lanes == rows + 8 * b, m[b], 0.0), axis=1, keepdims=True)
            parts.append(m[b][:, 64:] / jnp.sqrt(d))
        out.append(jnp.concatenate(parts, axis=0))
    return out


def kernel(
    g_ref, e_ref, w_ref, err_ref, p_ref, q_ref,
    st, xr, zs, zr, ys, yr, p1s, p1r, p2, p3, pf, qf,
    s1, r1, s2, r2, s3, r3, s4, r4, sx, rx, sz, rz, sy, ry, saz, raz, sax, rax,
):
    dp, tensor = lax.axis_index("dp"), lax.axis_index("tensor")
    z = lax.rem(dp, NZ)
    xa = lax.div(dp, NZ)
    x = lax.rem(xa, NX)
    yh = lax.div(xa, NX)
    yl, core = lax.div(tensor, 2), lax.rem(tensor, 2)
    y = yh * NYL + yl

    def at(yy, xx, zz, cc):
        return {"dp": (lax.div(yy, NYL) * NX + xx) * NZ + zz, "tensor": lax.rem(yy, NYL) * 2 + cc}

    def x_of(d):
        return lax.rem(x + d, NX)

    def z_of(d):
        return lax.rem(z + d, NZ)

    def y_of(d):
        return lax.rem(y + d, NY)

    def xc_peer(s):
        return at(y, x_of(s // 2), z, 1 - core if s % 2 else core)

    def x_peer(d):
        return at(y, x_of(d), z, core)

    def z_peer(d):
        return at(y, x, z_of(d), core)

    def y_peer(d):
        return at(y_of(d), x, z, core)

    def copy(src, dst, send, recv, to):
        c = pltpu.make_async_remote_copy(
            src_ref=src, dst_ref=dst, send_sem=send, recv_sem=recv, device_id=to, device_id_type=pl.DeviceIdType.MESH
        )
        c.start()
        return c

    barrier = pltpu.get_barrier_semaphore()
    peers = [xc_peer(s) for s in range(1, 8)] + [y_peer(d) for d in range(1, NY)] + [z_peer(d) for d in range(1, NZ)]
    for peer in peers:
        pl.semaphore_signal(barrier, inc=1, device_id=peer, device_id_type=pl.DeviceIdType.MESH)

    for xq in range(NX):
        st[xq * QU + UNITS : (xq + 1) * QU] = jnp.zeros((QU - UNITS, 8, 256), jnp.float32)
    for j in range(FD // 128):
        cols = slice(128 * j, 128 * j + 128)
        c = g_ref[:, cols].astype(jnp.float32) + e_ref[:, cols]
        err_ref[:, cols] = c
        t = c.T.reshape(16, 8, 256)
        for h in (2 * j, 2 * j + 1):
            base = (h // 7) * QU + (h % 7) * 8
            st[base : base + 8] = t[(h - 2 * j) * 8 : (h - 2 * j) * 8 + 8]
    for k in range(2):
        part = dot_nt(w_ref[64 * k : 64 * k + 64], err_ref[128 * k : 128 * k + 128])
        p1s[4 * k : 4 * k + 4] = part.reshape(4, 16, 128)

    pl.semaphore_wait(barrier, len(peers))

    owner = x * 2 + core
    c1 = []
    for s in range(1, 8):
        to = x_of(s // 2) * 2 + (1 - core if s % 2 else core)
        c1.append(copy(p1s.at[to], p1r.at[s], s1.at[s], r1.at[s], xc_peer(s)))

    cx = {}
    for i, off in enumerate(FAR_FIRST):
        zt = z_of(off)
        for d in (2, 1, 3):
            cx[d, off] = copy(
                st.at[pl.ds(x_of(d) * QU + zt * CH, CH)],
                xr.at[d - 1, pl.ds(off * CH, CH)],
                sx.at[d - 1, off], rx.at[d - 1, off], x_peer(d),
            )

    for c in c1:
        c.wait_recv()
    total = p1s[pl.ds(owner, 1)]
    for s in range(1, 8):
        total = total + p1r[s : s + 1]
    p2[pl.ds(y, 1)] = total
    c2 = [copy(p2.at[y], p2.at[y], s2.at[d], r2.at[d], y_peer(d)) for d in (4, 3, 5, 2, 6, 1, 7)]

    cz = {}

    def forward(off):
        for d in (1, 3, 2):
            cx[d, off].wait_recv()
        own = st[pl.ds(x * QU + z_of(off) * CH, CH)]
        here = slice(off * CH, off * CH + CH)
        zs[here] = (own + xr[0, here]) + (xr[1, here] + xr[2, here])
        if off:
            cz[off] = copy(zs.at[pl.ds(off * CH, CH)], zr.at[off], sz.at[off], rz.at[off], z_peer(off))

    for off in FAR_FIRST[:3]:
        forward(off)

    for c in c2:
        c.wait_recv()
    total = p2[0:1]
    for i in range(1, NY):
        total = total + p2[i : i + 1]
    p3[pl.ds(z, 1)] = total
    c3 = [copy(p3.at[z], p3.at[z], s3.at[d], r3.at[d], z_peer(d)) for d in FAR_FIRST[:-1]]

    for off in FAR_FIRST[3:8]:
        forward(off)

    for c in c3:
        c.wait_recv()
    total = p3[0:1]
    for i in range(1, NZ):
        total = total + p3[i : i + 1]
    pf[pl.ds(owner, 1)] = total
    c4 = [copy(pf.at[owner], pf.at[owner], s4.at[s], r4.at[s], xc_peer(s)) for s in range(1, 8)]

    for off in FAR_FIRST[8:]:
        forward(off)

    for c in c4:
        c.wait_recv()
    pt = pf[...].reshape(128, 128)
    pk = [pt[:64], pt[64:]]
    inv = inverse_factors([dot_nt(a, a) for a in pk])
    factor = jnp.concatenate([dot(inv[k], pk[k]) for k in range(2)], axis=0)
    p_ref[...] = factor
    flipped = factor.T
    lane = lax.broadcasted_iota(jnp.int32, (128, 128), 1)
    p_wide = jnp.concatenate([jnp.where(lane < 64, flipped, 0.0), jnp.where(lane < 64, 0.0, flipped)], axis=0)

    for off in FAR_FIRST[:-1]:
        cz[off].wait_recv()
    total = zs[0:CH]
    for off in range(1, NZ):
        total = total + zr[off]
    ys[...] = total
    cy = copy(ys, yr, sy, ry, y_peer(NYL))
    cy.wait_recv()
    summed = ys[...] + yr[...]

    mine = pl.ds(x * QU + z * CH, CH)
    qf[mine] = dot(summed.reshape(CH * 8, 256), p_wide).reshape(CH, 8, 128)
    caz = {off: copy(qf.at[mine], qf.at[mine], saz.at[off], raz.at[off], z_peer(off)) for off in FAR_FIRST[:-1]}
    cax = []

    def spread(off):
        piece = pl.ds(x * QU + z_of(NZ - off) * CH, CH)
        for d in (2, 1, 3):
            cax.append(copy(qf.at[piece], qf.at[piece], sax.at[d - 1, off], rax.at[d - 1, off], x_peer(d)))

    spread(0)
    for off in NEAR_FIRST:
        caz[off].wait_recv()
        spread(off)
    for c in cax:
        c.wait_recv()

    p_parts = halves(p_wide * (1.0 / (2 * NX * NZ)))
    for j in range(FD // 128):
        cols = slice(128 * j, 128 * j + 128)
        rows = []
        for h in (2 * j, 2 * j + 1):
            base = (h // 7) * QU + (h % 7) * 8
            rows.append(qf[base : base + 8].reshape(64, 128))
        qt = jnp.concatenate(rows, axis=0).T
        q_ref[:, cols] = qt
        err_ref[:, cols] = err_ref[:, cols] - dot3(p_parts, qt)

    for c in c1 + c2 + c3 + c4 + list(cx.values()) + list(cz.values()) + [cy] + list(caz.values()) + cax:
        c.wait_send()


def local(gradient, error_buffer, q_warm):
    g = gradient.reshape(256, FD)
    e = error_buffer.reshape(256, FD)
    w = jnp.swapaxes(q_warm, 1, 2).reshape(128, FD)
    f32 = jnp.float32
    dma = pltpu.SemaphoreType.DMA
    vmem = pl.BlockSpec(memory_space=pltpu.VMEM)
    err, pt, qt = pl.pallas_call(
        kernel,
        out_shape=(
            jax.ShapeDtypeStruct((256, FD), f32),
            jax.ShapeDtypeStruct((128, 128), f32),
            jax.ShapeDtypeStruct((128, FD), f32),
        ),
        in_specs=[vmem] * 3,
        out_specs=(vmem,) * 3,
        scratch_shapes=[
            pltpu.VMEM((NX * QU, 8, 256), f32),
            pltpu.VMEM((3, QU, 8, 256), f32),
            pltpu.VMEM((QU, 8, 256), f32),
            pltpu.VMEM((NZ, CH, 8, 256), f32),
            pltpu.VMEM((CH, 8, 256), f32),
            pltpu.VMEM((CH, 8, 256), f32),
            pltpu.VMEM((8, 16, 128), f32),
            pltpu.VMEM((8, 16, 128), f32),
            pltpu.VMEM((NY, 16, 128), f32),
            pltpu.VMEM((NZ, 16, 128), f32),
            pltpu.VMEM((8, 16, 128), f32),
            pltpu.VMEM((NX * QU, 8, 128), f32),
            dma((8,)), dma((8,)), dma((8,)), dma((8,)), dma((12,)), dma((12,)), dma((8,)), dma((8,)),
            dma((3, 12)), dma((3, 12)), dma((12,)), dma((12,)), dma, dma,
            dma((12,)), dma((12,)), dma((3, 12)), dma((3, 12)),
        ],
        compiler_params=pltpu.CompilerParams(
            collective_id=0, has_side_effects=True, vmem_limit_bytes=48 * 1024 * 1024
        ),
    )(g, e, w)
    p_factor = jnp.swapaxes(pt.reshape(2, 64, 128), 1, 2)
    q_factor = jnp.swapaxes(qt.reshape(2, 64, FD), 1, 2)
    return err.reshape(1, 2, 128, FD), p_factor, q_factor


def solution(mesh):
    in_specs = (
        P("dp", None, None, "tensor"),
        P("dp", None, None, "tensor"),
        P(None, "tensor", None),
    )
    out_specs = (P("dp", None, None, "tensor"), P(), P(None, "tensor", None))
    return jax.shard_map(local, mesh=mesh, in_specs=in_specs, out_specs=out_specs, check_vma=False)
```

time: 1700 us -> 89.4 us (0.05)
  the two profiles are of different devices: /device:TPU:56 before, /device:TPU:1 now
where the time goes in v1:
time: 89.4 us; the launch traced here: 89.2 us
  Pallas kernels  83.4 us (93%)
  local copies, waits for them, and re-layouts  5.13 us (6%)
    pallas_call x1, Pallas kernels, local(): pl.pallas_call(kernel, out_shape=(jax.ShapeDtypeStruct((256, FD), f32), j...  83.4 us
    unnamed x7, local copies, waits for them, and re-layouts  5.13 us

profile of v1, /device:TPU:1, one launch (start us, length us, event | category | flops | bytes accessed | tf_op | source)
XLA Modules:
  0.0 89.2 jit_solution(3500813730615838429)
XLA Ops:
  0.6 0.0 copy-start
  0.6 1.2 %copy-done = bf16[1,2,128,1792]{3,2,1,0:T(8,128)(2,1)S(1)} copy-done((bf16[1,2,128,1792]{3,2,1,0:T(8,128)(2,1)S(1)}, bf16[1,2,128,1792]{3,2,1,0:T(8,128)(2,1)}, u32[]{:S(2)}) %copy-start) | copy-done | bytes 917528
  1.8 0.0 copy-start.1
  1.8 1.2 %copy-done.1 = f32[2,1792,64]{1,2,0:T(8,128)S(1)} copy-done((f32[2,1792,64]{1,2,0:T(8,128)S(1)}, f32[2,1792,64]{1,2,0:T(8,128)}, u32[]{:S(2)}) %copy-start.1) | copy-done | bytes 917528
  3.0 83.4 %shard_map.58 = (f32[256,1792]{1,0:T(8,128)S(1)}, f32[128,128]{1,0:T(8,128)S(1)}, f32[128,1792]{1,0:T(8,128)S(1)}) custom-call(bf16[256,1792]{1,0:T(8,128)(2,1)S(1)} %bitcast.13, f32[256,1792]{1,0:T(8,128)} %bitcast.17, f32[128,1792]{1,0:T(8,128)S(1)} %bitcast.14), custom_call_target="tpu_custom_call" | custom-call | tf_op jit(solution)/shard_map/pallas_call | solution.py:256
  86.4 1.2 %copy.9 = f32[1,2,128,1792]{3,2,1,0:T(8,128)} copy(f32[1,2,128,1792]{3,2,1,0:T(8,128)S(1)} %bitcast.12) | data formatting | bytes 3670016
  87.6 0.6 copy.10
  88.2 0.9 %copy.11 = f32[2,1792,64]{1,2,0:T(8,128)} copy(f32[2,1792,64]{1,2,0:T(8,128)S(1)} %bitcast.15) | data formatting | bytes 1835008
Async XLA Ops:
  0.6 1.2 %copy-start = (bf16[1,2,128,1792]{3,2,1,0:T(8,128)(2,1)S(1)}, bf16[1,2,128,1792]{3,2,1,0:T(8,128)(2,1)}, u32[]{:S(2)}) copy-start(bf16[1,2,128,1792]{3,2,1,0:T(8,128)(2,1)} %param.3) | copy-start | bytes 2752516
  1.8 1.2 %copy-start.1 = (f32[2,1792,64]{1,2,0:T(8,128)S(1)}, f32[2,1792,64]{1,2,0:T(8,128)}, u32[]{:S(2)}) copy-start(f32[2,1792,64]{1,2,0:T(8,128)} %param.5) | copy-start | bytes 2752516

commit v2 on v1

v2 whole, which is shorter than its diff:
```python
import functools

import jax
import jax.numpy as jnp
from jax import lax
from jax.experimental import pallas as pl
from jax.experimental.pallas import tpu as pltpu
from jax.sharding import PartitionSpec as P

HI = lax.Precision.HIGHEST
NX, NZ, NYL = 4, 12, 4
NY = 2 * NYL
FD = 1792
UNITS = 56
CH = 5
QU = NZ * CH
FAR_FIRST = (6, 5, 7, 4, 8, 3, 9, 2, 10, 1, 11, 0)
NEAR_FIRST = (1, 11, 2, 10, 3, 9, 4, 8, 5, 7, 6)
NT = (((1,), (1,)), ((), ()))


def dot(a, b):
    return jnp.dot(a, b, precision=HI, preferred_element_type=jnp.float32)


def dot_nt(a, b):
    return lax.dot_general(a, b, NT, precision=HI, preferred_element_type=jnp.float32)


def halves(a):
    hi = a.astype(jnp.bfloat16)
    return hi, (a - hi.astype(jnp.float32)).astype(jnp.bfloat16)


def dot3(a, b):
    (ah, al), (bh, bl) = a, halves(b)
    f = functools.partial(jnp.dot, preferred_element_type=jnp.float32)
    return f(ah, bh) + (f(ah, bl) + f(al, bh))


def index_of(axis):
    return lax.broadcasted_iota(jnp.int32, (8, 128), axis)


def augmented(g):
    blocks = []
    for b in range(8):
        eye = jnp.where(index_of(1)[:, :64] == index_of(0)[:, :64] + 8 * b, 1.0, 0.0)
        blocks.append(jnp.concatenate([g[8 * b : 8 * b + 8], eye], axis=1))
    return blocks


def eliminate(ms):
    for jb in range(8):
        spread = [
            [[jnp.broadcast_to(m[b][:, j : j + 1], (8, 128)) for b in range(jb, 8)] for j in range(8 * jb, 8 * jb + 8)]
            for m in ms
        ]
        for ji in range(8):
            for m, columns in zip(ms, spread):
                column = columns[ji]
                pivot = 1.0 / column[0][ji : ji + 1]
                below = [jnp.where(index_of(0) > ji, column[0], 0.0)] + column[1:]
                for jj in range(ji + 1, 8):
                    factor = column[0][jj : jj + 1] * pivot
                    columns[jj] = [a - b * factor for a, b in zip(columns[jj], below)]
                row = m[jb][ji : ji + 1] * pivot
                for b in range(jb, 8):
                    m[b] = m[b] - below[b - jb] * row


def inverse_factor(m):
    parts = []
    for b in range(8):
        d = jnp.sum(jnp.where(index_of(1) == index_of(0) + 8 * b, m[b], 0.0), axis=1, keepdims=True)
        parts.append(m[b][:, 64:] / jnp.sqrt(d))
    return jnp.concatenate(parts, axis=0)


def kernel(
    c_ref, w_ref, p_ref, qf,
    st, xr, zs, zr, ys, yr, p1s, p1r, p2, p3, pf,
    s1, r1, sf, rf, s2, r2, s3, r3, s4, r4, sx, rx, sz, rz, sy, ry, saz, raz, sax, rax,
):
    dp, tensor = lax.axis_index("dp"), lax.axis_index("tensor")
    z = lax.rem(dp, NZ)
    xa = lax.div(dp, NZ)
    x = lax.rem(xa, NX)
    yh = lax.div(xa, NX)
    yl, core = lax.div(tensor, 2), lax.rem(tensor, 2)
    y = yh * NYL + yl

    def at(yy, xx, zz, cc):
        return {"dp": (lax.div(yy, NYL) * NX + xx) * NZ + zz, "tensor": lax.rem(yy, NYL) * 2 + cc}

    def x_of(d):
        return lax.rem(x + d, NX)

    def z_of(d):
        return lax.rem(z + d, NZ)

    def y_of(d):
        return lax.rem(y + d, NY)

    def xc_peer(s):
        return at(y, x_of(s // 2), z, 1 - core if s % 2 else core)

    def x_peer(d):
        return at(y, x_of(d), z, core)

    def z_peer(d):
        return at(y, x, z_of(d), core)

    def y_peer(d):
        return at(y_of(d), x, z, core)

    def copy(src, dst, send, recv, to):
        c = pltpu.make_async_remote_copy(
            src_ref=src, dst_ref=dst, send_sem=send, recv_sem=recv, device_id=to, device_id_type=pl.DeviceIdType.MESH
        )
        c.start()
        return c

    barrier = pltpu.get_barrier_semaphore()
    peers = [xc_peer(s) for s in range(1, 8)] + [y_peer(d) for d in range(1, NY)] + [z_peer(d) for d in range(1, NZ)]
    for peer in peers:
        pl.semaphore_signal(barrier, inc=1, device_id=peer, device_id_type=pl.DeviceIdType.MESH)

    for xq in range(NX):
        st[xq * QU + UNITS : (xq + 1) * QU] = jnp.zeros((QU - UNITS, 8, 256), jnp.float32)
    def runs(i):
        return [(h // 7) * QU + (h % 7) * 8 for h in range(4 * i, 4 * i + 4)]

    for i in range(FD // 256):
        t = c_ref[:, 256 * i : 256 * i + 256].T.reshape(32, 8, 256)
        for n, base in enumerate(runs(i)):
            st[base : base + 8] = t[8 * n : 8 * n + 8]

    pl.semaphore_wait(barrier, len(peers))

    cf, cx, cz = {}, {}, {}

    def cut(off):
        return 3 if FAR_FIRST.index(off) % 2 else 2

    def scatter(off):
        base, n = x_of(2) * QU + z_of(off) * CH, cut(off)
        cf[1, off] = copy(
            st.at[pl.ds(base, n)], xr.at[2, pl.ds(off * CH, n)], sf.at[0, off], rf.at[0, off], x_peer(1)
        )
        cf[3, off] = copy(
            st.at[pl.ds(base + n, CH - n)], xr.at[2, pl.ds(off * CH + n, CH - n)],
            sf.at[1, off], rf.at[1, off], x_peer(3),
        )

    def relay(off):
        n = cut(off)
        for d, lo, hi in ((1, 0, n), (3, n, CH)):
            base = x_of(d) * QU + z_of(off) * CH
            cf[d, off].wait_recv()
            there = pl.ds(base + lo, hi - lo)
            st[there] = st[there] + xr[2, off * CH + lo : off * CH + hi]
            cx[d, off] = copy(
                st.at[pl.ds(base, CH)], xr.at[d // 2, pl.ds(off * CH, CH)],
                sx.at[d // 2, off], rx.at[d // 2, off], x_peer(d),
            )

    def forward(off):
        for d in (1, 3):
            cx[d, off].wait_recv()
        own = st[pl.ds(x * QU + z_of(off) * CH, CH)]
        here = slice(off * CH, off * CH + CH)
        zs[here] = own + (xr[0, here] + xr[1, here])
        if off:
            cz[off] = copy(zs.at[pl.ds(off * CH, CH)], zr.at[off], sz.at[off], rz.at[off], z_peer(off))

    for off in FAR_FIRST[:2]:
        scatter(off)

    parts = [jnp.zeros((64, 128), jnp.float32)] * 2
    for i in range(FD // 256):
        t = jnp.concatenate([st[base : base + 8].reshape(64, 256) for base in runs(i)], axis=0)
        w = halves(w_ref[:, 256 * i : 256 * i + 256])
        for k in range(2):
            wk = [a[64 * k : 64 * k + 64] for a in w]
            parts[k] = parts[k] + dot3(wk, t[:, 128 * k : 128 * k + 128])
    for k in range(2):
        p1s[4 * k : 4 * k + 4] = parts[k].reshape(4, 16, 128)

    owner = x * 2 + core
    c1 = []
    for s in range(1, 8):
        to = x_of(s // 2) * 2 + (1 - core if s % 2 else core)
        c1.append(copy(p1s.at[to], p1r.at[s], s1.at[s], r1.at[s], xc_peer(s)))

    for off in FAR_FIRST[2:]:
        scatter(off)

    for c in c1:
        c.wait_recv()
    total = p1s[pl.ds(owner, 1)]
    for s in range(1, 8):
        total = total + p1r[s : s + 1]
    p3[pl.ds(z, 1)] = total
    c3 = [copy(p3.at[z], p3.at[z], s3.at[d], r3.at[d], z_peer(d)) for d in FAR_FIRST[:-1]]

    for off in FAR_FIRST[:3]:
        relay(off)
    for i in range(3, 7):
        relay(FAR_FIRST[i])
        forward(FAR_FIRST[i - 3])

    for c in c3:
        c.wait_recv()
    total = p3[0:1]
    for i in range(1, NZ):
        total = total + p3[i : i + 1]
    p2[pl.ds(y, 1)] = total
    c2 = [copy(p2.at[y], p2.at[y], s2.at[d], r2.at[d], y_peer(d)) for d in (4, 3, 5, 2, 6, 1, 7)]

    for i in range(7, 12):
        if i < NZ:
            relay(FAR_FIRST[i])
        forward(FAR_FIRST[i - 3])

    for c in c2:
        c.wait_recv()
    total = p2[0:1]
    for i in range(1, NY):
        total = total + p2[i : i + 1]
    pf[pl.ds(owner, 1)] = total
    c4 = [copy(pf.at[owner], pf.at[owner], s4.at[s], r4.at[s], xc_peer(s)) for s in range(1, 8)]

    for off in FAR_FIRST[9:]:
        forward(off)

    total = zs[0:CH]
    for off in FAR_FIRST[:-1]:
        cz[off].wait_recv()
        total = total + zr[off]
    ys[...] = total
    cy = copy(ys, yr, sy, ry, y_peer(NYL))

    for c in c4:
        c.wait_recv()
    pt = pf[...].reshape(128, 128)
    pk = [pt[:64], pt[64:]]
    ms = [augmented(dot_nt(a, a)) for a in pk]
    eliminate(ms)
    inv = [inverse_factor(m) for m in ms]
    factor = jnp.concatenate([dot(inv[k], pk[k]) for k in range(2)], axis=0)
    p_ref[...] = factor
    flipped = factor.T
    lane = lax.broadcasted_iota(jnp.int32, (128, 128), 1)
    p_wide = jnp.concatenate([jnp.where(lane < 64, flipped, 0.0), jnp.where(lane < 64, 0.0, flipped)], axis=0)

    cy.wait_recv()
    summed = ys[...] + yr[...]

    mine = pl.ds(x * QU + z * CH, CH)
    qf[mine] = dot(summed.reshape(CH * 8, 256), p_wide).reshape(CH, 8, 128)
    caz = {off: copy(qf.at[mine], qf.at[mine], saz.at[off], raz.at[off], z_peer(off)) for off in NEAR_FIRST}
    cax = []

    def spread(off):
        piece = pl.ds(x * QU + z_of(NZ - off) * CH, CH)
        for d in (2, 1, 3):
            cax.append(copy(qf.at[piece], qf.at[piece], sax.at[d - 1, off], rax.at[d - 1, off], x_peer(d)))

    spread(0)
    for off in NEAR_FIRST:
        caz[off].wait_recv()
        spread(off)
    for c in cax:
        c.wait_recv()

    for c in c1 + c2 + c3 + c4 + list(cf.values()) + list(cx.values()) + list(cz.values()) + [cy] + list(caz.values()) + cax:
        c.wait_send()


def last(c_ref, p_ref, qf, err_hbm, p_hbm, q_hbm, err, q, se, sp, sq):
    stores = [pltpu.make_async_copy(p_ref, p_hbm, sp)]
    stores[0].start()
    flipped = p_ref[...].T * (1.0 / (2 * NX * NZ))
    lane = lax.broadcasted_iota(jnp.int32, (128, 128), 1)
    wide = jnp.concatenate([jnp.where(lane < 64, flipped, 0.0), jnp.where(lane < 64, 0.0, flipped)], axis=0)
    p_parts = halves(wide)
    for i in range(FD // 256):
        cols = slice(256 * i, 256 * i + 256)
        rows = [(h // 7) * QU + (h % 7) * 8 for h in range(4 * i, 4 * i + 4)]
        qt = jnp.concatenate([qf[base : base + 8].reshape(64, 128) for base in rows], axis=0).T
        q[:, cols] = qt
        err[:, cols] = c_ref[:, cols] - dot3(p_parts, qt)
        there = pl.ds(256 * i, 256)
        stores.append(pltpu.make_async_copy(err.at[:, there], err_hbm.at[:, there], se.at[i]))
        stores.append(pltpu.make_async_copy(q.at[:, there], q_hbm.at[:, there], sq.at[i]))
        for c in stores[-2:]:
            c.start()
    for c in stores:
        c.wait()


def local(gradient, error_buffer, q_warm):
    c = (gradient.astype(jnp.float32) + error_buffer).reshape(256, FD)
    w = jnp.swapaxes(q_warm, 1, 2).reshape(128, FD)
    f32 = jnp.float32
    dma = pltpu.SemaphoreType.DMA
    vmem = pl.BlockSpec(memory_space=pltpu.VMEM)
    hbm = pl.BlockSpec(memory_space=pltpu.HBM)
    pt, qf = pl.pallas_call(
        kernel,
        out_shape=(
            jax.ShapeDtypeStruct((128, 128), f32),
            jax.ShapeDtypeStruct((NX * QU, 8, 128), f32),
        ),
        in_specs=[vmem] * 2,
        out_specs=(vmem,) * 2,
        scratch_shapes=[
            pltpu.VMEM((NX * QU, 8, 256), f32),
            pltpu.VMEM((3, QU, 8, 256), f32),
            pltpu.VMEM((QU, 8, 256), f32),
            pltpu.VMEM((NZ, CH, 8, 256), f32),
            pltpu.VMEM((CH, 8, 256), f32),
            pltpu.VMEM((CH, 8, 256), f32),
            pltpu.VMEM((8, 16, 128), f32),
            pltpu.VMEM((8, 16, 128), f32),
            pltpu.VMEM((NY, 16, 128), f32),
            pltpu.VMEM((NZ, 16, 128), f32),
            pltpu.VMEM((8, 16, 128), f32),
            dma((8,)), dma((8,)), dma((2, 12)), dma((2, 12)), dma((8,)), dma((8,)), dma((12,)), dma((12,)), dma((8,)), dma((8,)),
            dma((2, 12)), dma((2, 12)), dma((12,)), dma((12,)), dma, dma,
            dma((12,)), dma((12,)), dma((3, 12)), dma((3, 12)),
        ],
        compiler_params=pltpu.CompilerParams(
            collective_id=0, has_side_effects=True, vmem_limit_bytes=24 * 1024 * 1024
        ),
    )(c, w)
    err, pt, qt = pl.pallas_call(
        last,
        out_shape=(
            jax.ShapeDtypeStruct((256, FD), f32),
            jax.ShapeDtypeStruct((128, 128), f32),
            jax.ShapeDtypeStruct((128, FD), f32),
        ),
        in_specs=[vmem] * 3,
        out_specs=(hbm,) * 3,
        scratch_shapes=[pltpu.VMEM((256, FD), f32), pltpu.VMEM((128, FD), f32), dma((7,)), dma, dma((7,))],
        compiler_params=pltpu.CompilerParams(vmem_limit_bytes=16 * 1024 * 1024),
    )(c, pt, qf)
    p_factor = jnp.swapaxes(pt.reshape(2, 64, 128), 1, 2)
    q_factor = jnp.swapaxes(qt.reshape(2, 64, FD), 1, 2)
    return err.reshape(1, 2, 128, FD), p_factor, q_factor


def solution(mesh):
    in_specs = (
        P("dp", None, None, "tensor"),
        P("dp", None, None, "tensor"),
        P(None, "tensor", None),
    )
    out_specs = (P("dp", None, None, "tensor"), P(), P(None, "tensor", None))
    return jax.shard_map(local, mesh=mesh, in_specs=in_specs, out_specs=out_specs, check_vma=False)
```

time: 89.4 us -> 73.7 us (0.82)
  Pallas kernels: 83.4 us -> 70.3 us
  local copies, waits for them, and re-layouts: 5.13 us -> 0.03 us
  other arithmetic: 0 us -> 1.96 us
    pallas_call x1 -> x2, Pallas kernels: 83.4 us -> 70.3 us  [the longest x1 68.3 us: local(): pl.pallas_call(kernel, out_shape=(jax.ShapeDtypeStruct((128, 128), f32),...]
    unnamed x7 -> x2, local copies, waits for them, and re-layouts: 5.13 us -> 0.03 us
    add x0 -> x1, other arithmetic: none -> 1.96 us  [local(): c = (gradient.astype(jnp.float32) + error_buffer).reshape(256, FD)]
where the time goes in v2:
time: 73.7 us; the launch traced here: 72.9 us
  Pallas kernels  70.3 us (95%)
  other arithmetic  1.96 us (3%)
    pallas_call x1, Pallas kernels, local(): pl.pallas_call(kernel, out_shape=(jax.ShapeDtypeStruct((128, 128), f32),...  68.3 us
    add x1, other arithmetic, local(): c = (gradient.astype(jnp.float32) + error_buffer).reshape(256, FD)  1.96 us
    pallas_call x1, Pallas kernels, local(): pl.pallas_call(last, out_shape=(jax.ShapeDtypeStruct((256, FD), f32), jax...  1.95 us

profile of v2, /device:TPU:1, one launch (start us, length us, event | category | flops | bytes accessed | tf_op | source)
XLA Modules:
  0.0 72.9 jit_solution(2414138699968842367)
XLA Ops:
  0.6 0.0 copy-start
  0.6 2.0 %convert_add_fusion = f32[1,2,128,1792]{3,2,1,0:T(8,128)S(1)} fusion(f32[1,2,128,1792]{3,2,1,0:T(8,128)} %param.4, bf16[1,2,128,1792]{3,2,1,0:T(8,128)(2,1)} %param.3), kind=kLoop, calls=%fused_computation | loop fusion | flops 917504 | bytes 4587520 | tf_op jit(solution)/shard_map/add | solution.py:304
  2.6 0.0 copy-done
  2.6 68.3 %shard_map.58 = (f32[128,128]{1,0:T(8,128)S(1)}, f32[240,8,128]{2,1,0:T(8,128)S(1)}) custom-call(f32[256,1792]{1,0:T(8,128)S(1)} %bitcast.11, f32[128,1792]{1,0:T(8,128)S(1)} %bitcast.13), custom_call_target="tpu_custom_call" | custom-call | tf_op jit(solution)/shard_map/pallas_call | solution.py:310
  71.0 1.9 %shard_map.59 = (f32[256,1792]{1,0:T(8,128)}, f32[128,128]{1,0:T(8,128)}, f32[128,1792]{1,0:T(8,128)}) custom-call(f32[256,1792]{1,0:T(8,128)S(1)} %bitcast.12, f32[128,128]{1,0:T(8,128)S(1)} %get-tuple-element.8.p_ref, f32[240,8,128]{2,1,0:T(8,128)S(1)} %get-tuple-element.9.qf), custom_call_target="tpu_custom_call" | custom-call | tf_op jit(solution)/shard_map/pallas_call | solution.py:338
Async XLA Ops:
  0.6 2.0 %copy-start = (f32[2,1792,64]{1,2,0:T(8,128)S(1)}, f32[2,1792,64]{1,2,0:T(8,128)}, u32[]{:S(2)}) copy-start(f32[2,1792,64]{1,2,0:T(8,128)} %param.5) | copy-start | bytes 2752516

commit v3 on v2

--- a/solution.py
+++ b/solution.py
@@ -14,6 +14,7 @@
 UNITS = 56
 CH = 5
 QU = NZ * CH
+HALF = 2
 FAR_FIRST = (6, 5, 7, 4, 8, 3, 9, 2, 10, 1, 11, 0)
 NEAR_FIRST = (1, 11, 2, 10, 3, 9, 4, 8, 5, 7, 6)
 NT = (((1,), (1,)), ((), ()))
@@ -170,9 +171,24 @@
             cx[d, off].wait_recv()
         own = st[pl.ds(x * QU + z_of(off) * CH, CH)]
         here = slice(off * CH, off * CH + CH)
-        zs[here] = own + (xr[0, here] + xr[1, here])
-        if off:
-            cz[off] = copy(zs.at[pl.ds(off * CH, CH)], zr.at[off], sz.at[off], rz.at[off], z_peer(off))
+        total = own + (xr[0, here] + xr[1, here])
+        if off in (1, 2, 10, 11):
+            far = off + 3 if off < 6 else off - 3
+            cz[far].wait_recv()
+            total = total + zr[far]
+        zs[here] = total
+        if off in (3, 9):
+            lo, hi = (0, HALF) if off == 3 else (HALF, CH)
+            cz[6, off].wait_recv()
+            part = slice(off * CH + lo, off * CH + hi)
+            zs[part] = zs[part] + zr[6, lo:hi]
+        if off == 6:
+            for d, lo, hi, k in ((3, 0, HALF, 6), (9, HALF, CH, 0)):
+                src, dst = zs.at[pl.ds(off * CH + lo, hi - lo)], zr.at[6, pl.ds(lo, hi - lo)]
+                cz[6, d] = copy(src, dst, sz.at[k], rz.at[k], z_peer(d))
+        elif off:
+            to = 3 if off in (4, 5) else 9 if off in (7, 8) else off
+            cz[off] = copy(zs.at[pl.ds(off * CH, CH)], zr.at[off], sz.at[off], rz.at[off], z_peer(to))
 
     for off in FAR_FIRST[:2]:
         scatter(off)
@@ -235,7 +251,7 @@
         forward(off)
 
     total = zs[0:CH]
-    for off in FAR_FIRST[:-1]:
+    for off in (3, 9, 2, 10, 1, 11):
         cz[off].wait_recv()
         total = total + zr[off]
     ys[...] = total

time: 73.7 us -> 69.9 us (0.948)
  Pallas kernels: 70.3 us -> 66.4 us
    pallas_call x1, Pallas kernels: 68.3 us -> 64.4 us  [local(): pl.pallas_call(kernel, out_shape=(jax.ShapeDtypeStruct((128, 128), f32),...]
where the time goes in v3:
time: 69.9 us; the launch traced here: 69 us
  Pallas kernels  66.4 us (95%)
  other arithmetic  1.96 us (3%)
    pallas_call x1, Pallas kernels, local(): pl.pallas_call(kernel, out_shape=(jax.ShapeDtypeStruct((128, 128), f32),...  64.4 us
    add x1, other arithmetic, local(): c = (gradient.astype(jnp.float32) + error_buffer).reshape(256, FD)  1.96 us
    pallas_call x1, Pallas kernels, local(): pl.pallas_call(last, out_shape=(jax.ShapeDtypeStruct((256, FD), f32), jax...  1.95 us

profile of v3, /device:TPU:1, one launch (start us, length us, event | category | flops | bytes accessed | tf_op | source)
XLA Modules:
  0.0 69.0 jit_solution(14090269360659182649)
XLA Ops:
  0.6 0.0 copy-start
  0.6 2.0 %convert_add_fusion = f32[1,2,128,1792]{3,2,1,0:T(8,128)S(1)} fusion(f32[1,2,128,1792]{3,2,1,0:T(8,128)} %param.4, bf16[1,2,128,1792]{3,2,1,0:T(8,128)(2,1)} %param.3), kind=kLoop, calls=%fused_computation | loop fusion | flops 917504 | bytes 4587520 | tf_op jit(solution)/shard_map/add | solution.py:320
  2.6 0.0 copy-done
  2.6 64.4 %shard_map.58 = (f32[128,128]{1,0:T(8,128)S(1)}, f32[240,8,128]{2,1,0:T(8,128)S(1)}) custom-call(f32[256,1792]{1,0:T(8,128)S(1)} %bitcast.11, f32[128,1792]{1,0:T(8,128)S(1)} %bitcast.13), custom_call_target="tpu_custom_call" | custom-call | tf_op jit(solution)/shard_map/pallas_call | solution.py:326
  67.1 1.9 %shard_map.59 = (f32[256,1792]{1,0:T(8,128)}, f32[128,128]{1,0:T(8,128)}, f32[128,1792]{1,0:T(8,128)}) custom-call(f32[256,1792]{1,0:T(8,128)S(1)} %bitcast.12, f32[128,128]{1,0:T(8,128)S(1)} %get-tuple-element.8.p_ref, f32[240,8,128]{2,1,0:T(8,128)S(1)} %get-tuple-element.9.qf), custom_call_target="tpu_custom_call" | custom-call | tf_op jit(solution)/shard_map/pallas_call | solution.py:354
Async XLA Ops:
  0.6 2.0 %copy-start = (f32[2,1792,64]{1,2,0:T(8,128)S(1)}, f32[2,1792,64]{1,2,0:T(8,128)}, u32[]{:S(2)}) copy-start(f32[2,1792,64]{1,2,0:T(8,128)} %param.5) | copy-start | bytes 2752516
